TPU v7x, 512 devices: a whole 4x8x8 slice. The times are simulated.
512 devices in a mesh: hours: 64 (over z, x, core), region: 8 (over y).
Axes of the slice: x: 4, y: 8, z: 8, core: 2. Of those that a mesh axis runs over, the one named last changes fastest.
Arguments:
- availability: float32 [4096, 16, 1024], P('hours', None, 'region'), may hold values from 0.1 to 1
- demand: float32 [4096, 1024], P('hours', 'region'), may hold values from 2 to 72, as said below
- gen_cost: float32 [16, 1024], P(None, 'region'), may hold values from 0.05 to 1
- cap_cost: float32 [8, 2048], P('region', 'hours'), may hold values from 204.8 to 2048
- owner_map: int32 [8, 2048], P('region'), may hold values from 0 to 2047, each once within a row
- line_ends: int32 [2, 2048], P(None, 'region'), may hold values from 0 to 127
- line_limit: float32 [2048], P('region'), may hold values from 0.5 to 4
- cross_ends: int32 [2, 8, 256], P(None, 'region'), may hold values from 0 to 127
- cross_limit: float32 [8, 256], P('region'), may hold values from 0.5 to 4
- pair_counts: int32 [8, 8], P('region'), may hold values from 0 to 32, as said below
- store_node: int32 [2048], P('region'), may hold values from 0 to 127
- store_energy: float32 [2048], P('region'), may hold values from 0.02 to 0.4
- store_power: float32 [2048], P('region'), may hold values from 0.2 to 2
- price_start: float32 [4096, 1024], P('hours', 'region'), may hold values from -3 to 0.5
Outputs:
- dispatch: float32 [4096, 16, 1024], P('hours', None, 'region')
- capacity: float32 [8, 2048], P('region', 'hours')
- prices: float32 [4096, 1024], P('hours', 'region')
- charge_state: float32 [4096, 2048], P('hours', 'region')
Inputs may be any that keep to these rules, and one draw needn't show every extreme that they name: `demand`: loads are positive. `owner_map`: each row lists every capacity column of its region once. `pair_counts`: cross lines in use among the 32 slots of each ordered pair of regions; a region has none to itself; some pair uses all 32.
All inputs are finite; a program needn't handle non-finite values.
Results may differ from a plain program's by a relative error of at most 0.00018.
Values sent between devices are 32-bit elements; how exact they have to be, the bound alone decides.
A program may use at most 64 MiB of HBM per device.

v0:
```python
import jax
import jax.numpy as jnp
from jax import lax
from jax.sharding import PartitionSpec as P

ITERS = 4
epsilon = 1e-06
highest = lax.Precision.HIGHEST


def shifted(value, axis, steps):
    count = lax.axis_size(axis)
    pairs = [(source, (source + steps) % count) for source in range(count)]
    return lax.ppermute(value, axis, pairs)


def one_hot(indices, labels):
    return (indices[:, None] == labels[None, :]).astype(jnp.float32)


def to_owners(partial_value, owned_cols):
    summed = lax.psum(partial_value, "hours")
    return lax.dynamic_slice_in_dim(summed, lax.axis_index("hours") * owned_cols, owned_cols)


def spread_columns(capacity_bar):
    return lax.all_gather(capacity_bar, "hours", axis=0, tiled=True)


def body(
    availability,
    demand,
    gen_cost,
    cap_cost,
    owner_map,
    line_ends,
    line_limit,
    cross_ends,
    cross_limit,
    pair_counts,
    store_node,
    store_energy,
    store_power,
    price_start,
):
    hour_rows, tech_count, node_count = availability.shape
    region_count = lax.axis_size("region")
    slot_count = cross_limit.shape[1]
    slot_width = slot_count // region_count
    owned_cols = cap_cost.shape[1]
    owner_cols = owner_map[0]
    inverse = jnp.argsort(owner_cols)
    node_ids = jnp.arange(node_count, dtype=jnp.int32)
    line_inc = one_hot(line_ends[1], node_ids) - one_hot(line_ends[0], node_ids)
    store_map = one_hot(store_node, node_ids)
    leave_map = one_hot(cross_ends[0, 0], node_ids)
    slot_ids = jnp.arange(slot_count, dtype=jnp.int32)
    pair_of = slot_ids // slot_width
    region_ids = jnp.arange(region_count, dtype=jnp.int32)
    in_use = jnp.sum(
        jnp.where(pair_of[:, None] == region_ids[None, :], pair_counts[0][None, :], 0), axis=1
    )
    cross_bound = jnp.where(slot_ids % slot_width < in_use, cross_limit[0], 0.0)
    reach_map = one_hot(
        pair_of * node_count + cross_ends[1, 0],
        jnp.arange(region_count * node_count, dtype=jnp.int32),
    )
    column_costs = cap_cost[0]
    col_weight = to_owners(jnp.sum(availability, axis=0).reshape(-1)[owner_cols], owned_cols)
    dispatch = jnp.zeros_like(availability)
    capacity = jnp.zeros((owned_cols,), jnp.float32)
    inner_flow = jnp.zeros((hour_rows, line_limit.shape[0]), jnp.float32)
    cross_flow = jnp.zeros((hour_rows, slot_count), jnp.float32)
    mirror_flow = jnp.zeros((hour_rows, slot_count), jnp.float32)
    discharge = jnp.zeros((hour_rows, store_node.shape[0]), jnp.float32)
    charge = jnp.zeros((hour_rows, store_node.shape[0]), jnp.float32)
    prices = price_start
    cap_duals = jnp.zeros_like(availability)
    store_duals = jnp.zeros((hour_rows, store_node.shape[0]), jnp.float32)
    weight = jnp.float32(1.0)
    for iteration in range(ITERS):
        final_sweep = iteration == ITERS - 1
        primal_step = 0.5 / weight
        far_side = jnp.dot(
            lax.all_gather(prices, "region", axis=1, tiled=True), reach_map.T, precision=highest
        )
        if iteration == 0:
            next_duals = jnp.zeros_like(store_duals)
            cap_pull = jnp.zeros((owned_cols,), jnp.float32)
        else:
            next_row = shifted(store_duals[:1], "hours", -1)
            next_duals = jnp.concatenate([store_duals[1:], next_row], axis=0)
            cap_pull = to_owners(
                jnp.sum(availability * cap_duals, axis=0).reshape(-1)[owner_cols], owned_cols
            )
        dispatch_new = jnp.maximum(
            dispatch - primal_step * (gen_cost[None] + prices[:, None, :] + cap_duals), 0.0
        )
        capacity_new = jnp.maximum(
            capacity - (column_costs - cap_pull) / (weight * col_weight), 0.0
        )
        inner_new = jnp.clip(
            inner_flow - primal_step * jnp.dot(prices, line_inc.T, precision=highest),
            -line_limit,
            line_limit,
        )
        cross_new = jnp.clip(
            cross_flow - primal_step * (far_side - jnp.dot(prices, leave_map.T, precision=highest)),
            -cross_bound,
            cross_bound,
        )
        mirror_new = mirror_flow
        discharge_new = jnp.clip(
            discharge
            - primal_step * (jnp.dot(prices, store_map.T, precision=highest) + store_duals),
            -store_power,
            store_power,
        )
        charge_new = jnp.clip(charge - primal_step * (store_duals - next_duals), 0.0, store_energy)
        if not final_sweep:
            cap_change = capacity_new - capacity
            primal_sq = (
                jnp.sum((dispatch_new - dispatch) ** 2)
                + jnp.sum(cap_change**2)
                + jnp.sum((inner_new - inner_flow) ** 2)
                + jnp.sum((cross_new - cross_flow) ** 2)
                + jnp.sum((discharge_new - discharge) ** 2)
                + jnp.sum((charge_new - charge) ** 2)
            )
            primal_sum = lax.psum(primal_sq, ("hours", "region"))
        dispatch_bar = 2.0 * dispatch_new - dispatch
        capacity_bar = 2.0 * capacity_new - capacity
        inner_bar = 2.0 * inner_new - inner_flow
        cross_bar = 2.0 * cross_new - cross_flow
        discharge_bar = 2.0 * discharge_new - discharge
        charge_bar = 2.0 * charge_new - charge
        capacity_all = spread_columns(capacity_bar)
        cap_dense = capacity_all[inverse].reshape(tech_count, node_count)
        per_dest = jnp.dot(cross_bar, reach_map, precision=highest)
        balance = (
            jnp.sum(dispatch_bar, axis=1)
            + jnp.dot(inner_bar, line_inc, precision=highest)
            + (
                lax.psum_scatter(per_dest, "region", scatter_dimension=1, tiled=True)
                - jnp.dot(cross_bar, leave_map, precision=highest)
            )
            + jnp.dot(discharge_bar, store_map, precision=highest)
            - demand
        )
        prev_row = shifted(charge_bar[-1:], "hours", 1)
        storage_rows = (
            charge_bar - jnp.concatenate([prev_row, charge_bar[:-1]], axis=0) + discharge_bar
        )
        cap_rows = dispatch_bar - availability * cap_dense[None]
        prices_new = prices + weight / (tech_count + 8.0) * balance
        cap_new = jnp.maximum(cap_duals + weight / 2.0 * cap_rows, 0.0)
        store_new = store_duals + weight / 3.0 * storage_rows
        if not final_sweep:
            dual_sq = (
                jnp.sum((prices_new - prices) ** 2)
                + jnp.sum((cap_new - cap_duals) ** 2)
                + jnp.sum((store_new - store_duals) ** 2)
            )
            dual_sum = lax.psum(dual_sq, ("hours", "region"))
            weight = jnp.sqrt(weight * jnp.sqrt((dual_sum + epsilon) / (primal_sum + epsilon)))
        dispatch, capacity, inner_flow, cross_flow = (
            dispatch_new,
            capacity_new,
            inner_new,
            cross_new,
        )
        mirror_flow = mirror_new
        discharge, charge = (discharge_new, charge_new)
        prices, cap_duals, store_duals = (prices_new, cap_new, store_new)
    return (dispatch, capacity[None], prices, charge)


def solution(mesh):
    placed = (
        P("hours", None, "region"),
        P("hours", "region"),
        P(None, "region"),
        P("region", "hours"),
        P("region", None),
        P(None, "region"),
        P("region"),
        P(None, "region", None),
        P("region", None),
        P("region", None),
        P("region"),
        P("region"),
        P("region"),
        P("hours", "region"),
    )
    return jax.shard_map(
        body,
        mesh=mesh,
        in_specs=placed,
        out_specs=(
            P("hours", None, "region"),
            P("region", "hours"),
            P("hours", "region"),
            P("hours", "region"),
        ),
        check_vma=False,
    )
```

profile of v0, /device:TPU:2, one launch (start us, length us, event | category | flops | bytes accessed | tf_op | source)
XLA Modules:
  0.0 1496.5 jit_solution(16780039333863139814)
XLA Ops:
  10.0 26.6 %all_gather.21 = f32[64,1024]{1,0:T(8,128)S(1)} all-gather(f32[64,128]{1,0:T(8,128)} %param.27), channel_id=1, replica_groups=mesh['hours'=64,'region'=8] {'region'}, dimensions={1}, use_global_device_ids=true | all-gather | bytes 294912 | tf_op jit(solution)/shard_map/all_gather | solution.py:85
  41.2 11.8 gather_fusion
  53.0 126.8 %psum.70 = f32[2048]{0:T(1024)S(1)} all-reduce(f32[2048]{0:T(1024)S(1)} %gather_fusion), channel_id=1, replica_groups=mesh['hours'=64,'region'=8] {'hours'}, use_global_device_ids=true, to_apply=%region_5.6 | all-reduce | flops 2048 | bytes 16384 | tf_op jit(solution)/shard_map/psum | solution.py:22
  182.5 126.4 %all-reduce = f32[2048]{0:T(1024)S(1)} all-reduce(f32[2048]{0:T(1024)S(1)} %multiply_dynamic-update-slice_fusion), channel_id=1, replica_groups=mesh['hours'=64,'region'=8] {'hours'}, use_global_device_ids=true, to_apply=%add | all-reduce | flops 2048 | bytes 16384
  308.9 5.0 sort.17
  314.0 11.8 gather_fusion.1
  326.8 11.8 gather_fusion.2
  340.6 126.1 %psum.73 = f32[2048]{0:T(1024)S(1)} all-reduce(f32[2048]{0:T(1024)S(1)} %gather_fusion.2), channel_id=1, replica_groups=mesh['hours'=64,'region'=8] {'hours'}, use_global_device_ids=true, to_apply=%region_21.22 | all-reduce | flops 2048 | bytes 16384 | tf_op jit(solution)/shard_map/psum | solution.py:22
  476.0 7.0 collective-permute-start.1
  483.0 95.3 %all-reduce.5 = (f32[]{:T(128)}, f32[]{:T(128)}) all-reduce(f32[]{:T(128)S(6)} %add.309, f32[]{:T(128)S(6)} %add.315), channel_id=1, replica_groups=mesh['hours'=64,'region'=8] {'hours','region'}, use_global_device_ids=true, to_apply=%region_9.10 | all-reduce | flops 2 | bytes 16 | tf_op jit(solution)/shard_map/psum | solution.py:164
  579.7 24.8 %all_gather.23 = f32[64,1024]{1,0:T(8,128)S(1)} all-gather(f32[64,128]{1,0:T(8,128)S(1)} %get-tuple-element.56), channel_id=1, replica_groups=mesh['hours'=64,'region'=8] {'region'}, dimensions={1}, use_global_device_ids=true | all-gather | bytes 294912 | tf_op jit(solution)/shard_map/all_gather | solution.py:85
  606.4 120.4 %all-reduce.1 = f32[2048]{0:T(1024)S(1)} all-reduce(f32[2048]{0:T(1024)S(1)} %subtract_dynamic-update-slice_fusion.1), channel_id=1, replica_groups=mesh['hours'=64,'region'=8] {'hours'}, use_global_device_ids=true, to_apply=%add.1 | all-reduce | flops 2048 | bytes 16384
  726.8 11.8 gather_fusion.3
  744.2 11.8 gather_fusion.4
  758.2 131.1 %psum.76 = f32[2048]{0:T(1024)S(1)} all-reduce(f32[2048]{0:T(1024)S(1)} %gather_fusion.4), channel_id=1, replica_groups=mesh['hours'=64,'region'=8] {'hours'}, use_global_device_ids=true, to_apply=%region_36.37 | all-reduce | flops 2048 | bytes 16384 | tf_op jit(solution)/shard_map/psum | solution.py:22
  900.0 100.8 %all-reduce.4 = (f32[]{:T(128)}, f32[]{:T(128)}) all-reduce(f32[]{:T(128)S(6)} %add.329, f32[]{:T(128)S(6)} %add.335), channel_id=1, replica_groups=mesh['hours'=64,'region'=8] {'hours','region'}, use_global_device_ids=true, to_apply=%region_24.25 | all-reduce | flops 2 | bytes 16 | tf_op jit(solution)/shard_map/psum | solution.py:164
  1003.9 24.8 %all_gather.25 = f32[64,1024]{1,0:T(8,128)S(1)} all-gather(f32[64,128]{1,0:T(8,128)S(1)} %get-tuple-element.63), channel_id=1, replica_groups=mesh['hours'=64,'region'=8] {'region'}, dimensions={1}, use_global_device_ids=true | all-gather | bytes 294912 | tf_op jit(solution)/shard_map/all_gather | solution.py:85
  1029.5 120.4 %all-reduce.2 = f32[2048]{0:T(1024)S(1)} all-reduce(f32[2048]{0:T(1024)S(1)} %subtract_dynamic-update-slice_fusion), channel_id=1, replica_groups=mesh['hours'=64,'region'=8] {'hours'}, use_global_device_ids=true, to_apply=%add.2 | all-reduce | flops 2048 | bytes 16384
  1149.9 11.8 gather_fusion.5
  1168.1 11.8 gather_fusion.6
  1180.2 131.1 %psum.79 = f32[2048]{0:T(1024)S(1)} all-reduce(f32[2048]{0:T(1024)S(1)} %gather_fusion.6), channel_id=1, replica_groups=mesh['hours'=64,'region'=8] {'hours'}, use_global_device_ids=true, to_apply=%region_48.49 | all-reduce | flops 2048 | bytes 16384 | tf_op jit(solution)/shard_map/psum | solution.py:22
  1321.9 100.9 %all-reduce.3 = (f32[]{:T(128)}, f32[]{:T(128)}) all-reduce(f32[]{:T(128)S(6)} %add.349, f32[]{:T(128)S(6)} %add.355), channel_id=1, replica_groups=mesh['hours'=64,'region'=8] {'hours','region'}, use_global_device_ids=true, to_apply=%region_39.40 | all-reduce | flops 2 | bytes 16 | tf_op jit(solution)/shard_map/psum | solution.py:164
  1424.3 24.8 %all_gather.27 = f32[64,1024]{1,0:T(8,128)S(1)} all-gather(f32[64,128]{1,0:T(8,128)S(1)} %get-tuple-element.70), channel_id=1, replica_groups=mesh['hours'=64,'region'=8] {'region'}, dimensions={1}, use_global_device_ids=true | all-gather | bytes 294912 | tf_op jit(solution)/shard_map/all_gather | solution.py:85
  1455.2 32.9 %reduce-scatter.11.cloned.1.call-done = f32[64,128]{1,0:T(8,128)} async-done(((f32[64,1024]{1,0:T(8,128)}), f32[64,128]{1,0:T(8,128)}) %reduce-scatter.11.cloned.1.call-update) | async-done | bytes 32784 | tf_op jit(solution)/shard_map/reduce_scatter | solution.py:144
  (126 shorter events, 52.3 us)
Async XLA Ops:
  7.2 465.0 %reduce-scatter.5.cloned.1.call-start = ((), (), s32[]{:S(2)}) async-start(), calls=%async_computation.4 | async-start | bytes 294912 | tf_op jit(solution)/shard_map/reduce_scatter | solution.py:144
  7.9 2.1 copy-start.9
  7.9 461.4 %collective-permute-start = (f32[1,256]{1,0:T(1,128)S(1)}, f32[1,256]{1,0:T(1,128)S(1)}, u32[]{:S(2)}, u32[]{:S(2)}) collective-permute-start(f32[1,256]{1,0:T(1,128)S(1)} %bitcast.122), channel_id=1, source_target_pairs={{0,8},{8,16},{16,24},{24,32},{32,40},{40,48},{48,56},{56,64},{64,7... | collective-permute-start | bytes 3080 | tf_op jit(solution)/shard_map/ppermute | solution.py:14
  36.6 0.7 copy-start.13
  36.6 0.7 copy-start.12
  37.2 0.8 copy-start.1
  37.3 3.8 copy-start
  40.3 853.9 %reduce-scatter.7.cloned.1.call-start = ((), (), s32[]{:S(2)}) async-start(), calls=%async_computation.5 | async-start | bytes 294912 | tf_op jit(solution)/shard_map/reduce_scatter | solution.py:144
  40.3 0.7 copy-start.11
  40.3 0.7 copy-start.5
  40.4 0.7 copy-start.10
  181.0 0.7 copy-start.8
  314.0 11.8 copy-start.3
  340.6 126.1 %copy-start.7 = (f32[256]{0:T(256)S(1)}, f32[256]{0:T(256)}, u32[]{:S(2)}) copy-start(f32[256]{0:T(256)} %param.26) | copy-start | bytes 3076
  469.2 0.7 copy-start.4
  472.1 1.1 copy-start.2
  476.0 262.6 %collective-permute-start.1 = (f32[1,256]{1,0:T(1,128)S(1)}, f32[1,256]{1,0:T(1,128)S(1)}, u32[]{:S(2)}, u32[]{:S(2)}) collective-permute-start(f32[1,256]{1,0:T(1,128)S(1)} %slice.79), channel_id=1, source_target_pairs={{0,504},{8,0},{16,8},{24,16},{32,24},{40,32},{48,40},{56,48},{64,5... | collective-permute-start | bytes 3080 | tf_op jit(solution)/shard_map/ppermute | solution.py:14
  738.6 0.7 copy-start.6
  742.9 573.2 %reduce-scatter.9.cloned.1.call-start = ((), (), s32[]{:S(2)}) async-start(), calls=%async_computation.6 | async-start | bytes 294912 | tf_op jit(solution)/shard_map/reduce_scatter | solution.py:144
  756.0 135.9 %collective-permute-start.2 = (f32[1,256]{1,0:T(1,128)S(1)}, f32[1,256]{1,0:T(1,128)S(1)}, u32[]{:S(2)}, u32[]{:S(2)}) collective-permute-start(f32[1,256]{1,0:T(1,128)S(1)} %slice.80), channel_id=1, source_target_pairs={{0,8},{8,16},{16,24},{24,32},{32,40},{40,48},{48,56},{56,64},{64,7... | collective-permute-start | bytes 3080 | tf_op jit(solution)/shard_map/ppermute | solution.py:14
  898.0 130.7 %collective-permute-start.3 = (f32[1,256]{1,0:T(1,128)S(1)}, f32[1,256]{1,0:T(1,128)S(1)}, u32[]{:S(2)}, u32[]{:S(2)}) collective-permute-start(f32[1,256]{1,0:T(1,128)S(1)} %slice.83), channel_id=1, source_target_pairs={{0,504},{8,0},{16,8},{24,16},{32,24},{40,32},{48,40},{56,48},{64,5... | collective-permute-start | bytes 3080 | tf_op jit(solution)/shard_map/ppermute | solution.py:14
  1161.7 152.2 %collective-permute-start.4 = (f32[1,256]{1,0:T(1,128)S(1)}, f32[1,256]{1,0:T(1,128)S(1)}, u32[]{:S(2)}, u32[]{:S(2)}) collective-permute-start(f32[1,256]{1,0:T(1,128)S(1)} %slice.84), channel_id=1, source_target_pairs={{0,8},{8,16},{16,24},{24,32},{32,40},{40,48},{48,56},{56,64},{64,7... | collective-permute-start | bytes 3080 | tf_op jit(solution)/shard_map/ppermute | solution.py:14
  1166.6 321.5 %reduce-scatter.11.cloned.1.call-start = ((), (), s32[]{:S(2)}) async-start(), calls=%async_computation.7 | async-start | bytes 294912 | tf_op jit(solution)/shard_map/reduce_scatter | solution.py:144
  1320.0 134.3 %collective-permute-start.5 = (f32[1,256]{1,0:T(1,128)S(1)}, f32[1,256]{1,0:T(1,128)S(1)}, u32[]{:S(2)}, u32[]{:S(2)}) collective-permute-start(f32[1,256]{1,0:T(1,128)S(1)} %slice.87), channel_id=1, source_target_pairs={{0,504},{8,0},{16,8},{24,16},{32,24},{40,32},{48,40},{56,48},{64,5... | collective-permute-start | bytes 3080 | tf_op jit(solution)/shard_map/ppermute | solution.py:14
Sparse Core Ops, SparseCore 0:
  40.4 42.1 reduce-scatter.4
  743.0 39.1 reduce-scatter.6
  1166.7 41.5 reduce-scatter.8
  1453.5 34.5 reduce-scatter.10
where the time goes:
time: 1500 us
  blocking collectives  1280 us (85%)
  local copies, waits for them, and re-layouts  86.5 us (6%)
  between operations  36.6 us (2%)
  waiting for transfers between devices  33 us (2%)
  matrix products  26.5 us (2%)
  starting transfers between devices  16.8 us (1%)
  other arithmetic  16.8 us (1%)
    psum x4, blocking collectives, to_owners(): summed = lax.psum(partial_value, 'hours')  515 us
    unnamed x3, blocking collectives  367 us
    psum x3, blocking collectives, body(): dual_sum = lax.psum(dual_sq, ('hours', 'region'))  297 us
    all_gather x4, blocking collectives, body(): lax.all_gather(prices, 'region', axis=1, tiled=True)  101 us
    gather x3, local copies, waits for them, and re-layouts, body(): cap_dense = capacity_all[inverse].reshape(tech_count, node_count)  35.3 us
    gather x3, local copies, waits for them, and re-layouts, body(): jnp.sum(availability * cap_duals, axis=0).reshape(-1)[owner_cols]  35.3 us
    reduce_scatter x4, waiting for transfers between devices, body(): lax.psum_scatter(per_dest, 'region', scatter_dimension=1, tiled=True)  32.9 us
  transfers between devices with their start and end apart: 10, of which 1 were waited for; matrix products, arithmetic and copies ran while one was open for 7% of the time, Pallas kernels for 0%

commit v1 on v0

--- a/solution.py
+++ b/solution.py
@@ -6,6 +6,11 @@
 ITERS = 4
 epsilon = 1e-06
 highest = lax.Precision.HIGHEST
+
+
+def add_all(array, mesh_axis):
+    parts = lax.all_gather(array, mesh_axis)
+    return jnp.sum(parts, axis=0)
 
 
 def shifted(value, axis, steps):
@@ -161,7 +166,7 @@
                 + jnp.sum((cap_new - cap_duals) ** 2)
                 + jnp.sum((store_new - store_duals) ** 2)
             )
-            dual_sum = lax.psum(dual_sq, ("hours", "region"))
+            dual_sum = add_all(dual_sq, ("hours", "region"))
             weight = jnp.sqrt(weight * jnp.sqrt((dual_sum + epsilon) / (primal_sum + epsilon)))
         dispatch, capacity, inner_flow, cross_flow = (
             dispatch_new,

time: 1500 us -> 1500 us (level)
    psum x3 -> x0, blocking collectives: 297 us -> none  [body(): dual_sum = lax.psum(dual_sq, ('hours', 'region'))]
    unnamed x3 -> x6, blocking collectives: 367 us -> 664 us
where the time goes in v1:
time: 1500 us
  blocking collectives  1280 us (85%)
  local copies, waits for them, and re-layouts  86.8 us (6%)
  between operations  36.6 us (2%)
  waiting for transfers between devices  32.9 us (2%)
  matrix products  26.5 us (2%)
  other arithmetic  18.6 us (1%)
  starting transfers between devices  16.8 us (1%)
    unnamed x6, blocking collectives  664 us
    psum x4, blocking collectives, to_owners(): summed = lax.psum(partial_value, 'hours')  515 us
    all_gather x4, blocking collectives, body(): lax.all_gather(prices, 'region', axis=1, tiled=True)  101 us
    gather x3, local copies, waits for them, and re-layouts, body(): cap_dense = capacity_all[inverse].reshape(tech_count, node_count)  35.3 us
    gather x3, local copies, waits for them, and re-layouts, body(): jnp.sum(availability * cap_duals, axis=0).reshape(-1)[owner_cols]  35.3 us
    reduce_scatter x4, waiting for transfers between devices, body(): lax.psum_scatter(per_dest, 'region', scatter_dimension=1, tiled=True)  32.8 us
  transfers between devices with their start and end apart: 10, of which 1 were waited for; matrix products, arithmetic and copies ran while one was open for 7% of the time, Pallas kernels for 0%

profile of v1, /device:TPU:2, one launch (start us, length us, event | category | flops | bytes accessed | tf_op | source)
XLA Modules:
  0.0 1498.5 jit_solution(12454229993629076851)
XLA Ops:
  10.0 26.6 %all_gather.39 = f32[64,1024]{1,0:T(8,128)S(1)} all-gather(f32[64,128]{1,0:T(8,128)} %param.27), channel_id=1, replica_groups=mesh['hours'=64,'region'=8] {'region'}, dimensions={1}, use_global_device_ids=true | all-gather | bytes 294912 | tf_op jit(solution)/shard_map/all_gather | solution.py:90
  41.2 11.8 gather_fusion
  53.0 126.8 %psum.49 = f32[2048]{0:T(1024)S(1)} all-reduce(f32[2048]{0:T(1024)S(1)} %gather_fusion), channel_id=1, replica_groups=mesh['hours'=64,'region'=8] {'hours'}, use_global_device_ids=true, to_apply=%region_5.6 | all-reduce | flops 2048 | bytes 16384 | tf_op jit(solution)/shard_map/psum | solution.py:27
  182.5 126.4 %all-reduce = f32[2048]{0:T(1024)S(1)} all-reduce(f32[2048]{0:T(1024)S(1)} %multiply_dynamic-update-slice_fusion), channel_id=1, replica_groups=mesh['hours'=64,'region'=8] {'hours'}, use_global_device_ids=true, to_apply=%add | all-reduce | flops 2048 | bytes 16384
  308.9 5.0 sort.17
  314.0 11.8 gather_fusion.1
  326.8 11.8 gather_fusion.2
  340.6 126.1 %psum.51 = f32[2048]{0:T(1024)S(1)} all-reduce(f32[2048]{0:T(1024)S(1)} %gather_fusion.2), channel_id=1, replica_groups=mesh['hours'=64,'region'=8] {'hours'}, use_global_device_ids=true, to_apply=%region_21.22 | all-reduce | flops 2048 | bytes 16384 | tf_op jit(solution)/shard_map/psum | solution.py:27
  470.9 7.0 collective-permute-start.1
  483.1 95.2 %all-reduce.8 = (f32[512]{0:T(512)S(1)}, f32[]{:T(128)}) all-reduce(f32[512]{0:T(512)S(1)} %dynamic-update-slice.1, f32[]{:T(128)S(6)} %add.309), channel_id=1, replica_groups=mesh['hours'=64,'region'=8] {'hours','region'}, use_global_device_ids=true, to_apply=%add.1 | all-reduce | flops 513 | bytes 4104
  580.4 24.8 %all_gather.43 = f32[64,1024]{1,0:T(8,128)S(1)} all-gather(f32[64,128]{1,0:T(8,128)S(1)} %get-tuple-element.56), channel_id=1, replica_groups=mesh['hours'=64,'region'=8] {'region'}, dimensions={1}, use_global_device_ids=true | all-gather | bytes 294912 | tf_op jit(solution)/shard_map/all_gather | solution.py:90
  607.0 120.4 %all-reduce.2 = f32[2048]{0:T(1024)S(1)} all-reduce(f32[2048]{0:T(1024)S(1)} %subtract_dynamic-update-slice_fusion.1), channel_id=1, replica_groups=mesh['hours'=64,'region'=8] {'hours'}, use_global_device_ids=true, to_apply=%add.2 | all-reduce | flops 2048 | bytes 16384
  727.5 11.8 gather_fusion.3
  744.9 11.8 gather_fusion.4
  758.9 131.1 %psum.53 = f32[2048]{0:T(1024)S(1)} all-reduce(f32[2048]{0:T(1024)S(1)} %gather_fusion.4), channel_id=1, replica_groups=mesh['hours'=64,'region'=8] {'hours'}, use_global_device_ids=true, to_apply=%region_36.37 | all-reduce | flops 2048 | bytes 16384 | tf_op jit(solution)/shard_map/psum | solution.py:27
  900.8 100.7 %all-reduce.7 = (f32[512]{0:T(512)S(1)}, f32[]{:T(128)}) all-reduce(f32[512]{0:T(512)S(1)} %dynamic-update-slice.3, f32[]{:T(128)S(6)} %add.329), channel_id=1, replica_groups=mesh['hours'=64,'region'=8] {'hours','region'}, use_global_device_ids=true, to_apply=%add.3 | all-reduce | flops 513 | bytes 4104
  1005.3 24.8 %all_gather.47 = f32[64,1024]{1,0:T(8,128)S(1)} all-gather(f32[64,128]{1,0:T(8,128)S(1)} %get-tuple-element.63), channel_id=1, replica_groups=mesh['hours'=64,'region'=8] {'region'}, dimensions={1}, use_global_device_ids=true | all-gather | bytes 294912 | tf_op jit(solution)/shard_map/all_gather | solution.py:90
  1030.9 120.4 %all-reduce.4 = f32[2048]{0:T(1024)S(1)} all-reduce(f32[2048]{0:T(1024)S(1)} %subtract_dynamic-update-slice_fusion), channel_id=1, replica_groups=mesh['hours'=64,'region'=8] {'hours'}, use_global_device_ids=true, to_apply=%add.4 | all-reduce | flops 2048 | bytes 16384
  1151.3 11.8 gather_fusion.5
  1169.5 11.8 gather_fusion.6
  1181.6 131.1 %psum.55 = f32[2048]{0:T(1024)S(1)} all-reduce(f32[2048]{0:T(1024)S(1)} %gather_fusion.6), channel_id=1, replica_groups=mesh['hours'=64,'region'=8] {'hours'}, use_global_device_ids=true, to_apply=%region_48.49 | all-reduce | flops 2048 | bytes 16384 | tf_op jit(solution)/shard_map/psum | solution.py:27
  1323.4 100.9 %all-reduce.6 = (f32[512]{0:T(512)S(1)}, f32[]{:T(128)}) all-reduce(f32[512]{0:T(512)S(1)} %dynamic-update-slice.5, f32[]{:T(128)S(6)} %add.349), channel_id=1, replica_groups=mesh['hours'=64,'region'=8] {'hours','region'}, use_global_device_ids=true, to_apply=%add.5 | all-reduce | flops 513 | bytes 4104
  1426.4 24.8 %all_gather.51 = f32[64,1024]{1,0:T(8,128)S(1)} all-gather(f32[64,128]{1,0:T(8,128)S(1)} %get-tuple-element.70), channel_id=1, replica_groups=mesh['hours'=64,'region'=8] {'region'}, dimensions={1}, use_global_device_ids=true | all-gather | bytes 294912 | tf_op jit(solution)/shard_map/all_gather | solution.py:90
  1457.3 32.8 %reduce-scatter.11.cloned.1.call-done = f32[64,128]{1,0:T(8,128)} async-done(((f32[64,1024]{1,0:T(8,128)}), f32[64,128]{1,0:T(8,128)}) %reduce-scatter.11.cloned.1.call-update) | async-done | bytes 32784 | tf_op jit(solution)/shard_map/reduce_scatter | solution.py:149
  (135 shorter events, 54.4 us)
Async XLA Ops:
  7.2 472.0 %reduce-scatter.5.cloned.1.call-start = ((), (), s32[]{:S(2)}) async-start(), calls=%async_computation.4 | async-start | bytes 294912 | tf_op jit(solution)/shard_map/reduce_scatter | solution.py:149
  7.9 2.1 copy-start.9
  7.9 461.4 %collective-permute-start = (f32[1,256]{1,0:T(1,128)S(1)}, f32[1,256]{1,0:T(1,128)S(1)}, u32[]{:S(2)}, u32[]{:S(2)}) collective-permute-start(f32[1,256]{1,0:T(1,128)S(1)} %bitcast.125), channel_id=1, source_target_pairs={{0,8},{8,16},{16,24},{24,32},{32,40},{40,48},{48,56},{56,64},{64,7... | collective-permute-start | bytes 3080 | tf_op jit(solution)/shard_map/ppermute | solution.py:19
  36.6 0.7 copy-start.13
  36.6 0.7 copy-start.12
  37.2 0.8 copy-start.1
  37.3 3.8 copy-start
  40.3 856.5 %reduce-scatter.7.cloned.1.call-start = ((), (), s32[]{:S(2)}) async-start(), calls=%async_computation.5 | async-start | bytes 294912 | tf_op jit(solution)/shard_map/reduce_scatter | solution.py:149
  40.3 0.7 copy-start.11
  40.3 0.7 copy-start.5
  40.4 0.7 copy-start.10
  181.0 0.7 copy-start.8
  314.0 11.8 copy-start.3
  340.6 126.1 %copy-start.7 = (f32[256]{0:T(256)S(1)}, f32[256]{0:T(256)}, u32[]{:S(2)}) copy-start(f32[256]{0:T(256)} %param.26) | copy-start | bytes 3076
  469.2 0.7 copy-start.4
  470.9 268.4 %collective-permute-start.1 = (f32[1,256]{1,0:T(1,128)S(1)}, f32[1,256]{1,0:T(1,128)S(1)}, u32[]{:S(2)}, u32[]{:S(2)}) collective-permute-start(f32[1,256]{1,0:T(1,128)S(1)} %slice.79), channel_id=1, source_target_pairs={{0,504},{8,0},{16,8},{24,16},{32,24},{40,32},{48,40},{56,48},{64,5... | collective-permute-start | bytes 3080 | tf_op jit(solution)/shard_map/ppermute | solution.py:19
  479.1 1.1 copy-start.2
  739.3 0.7 copy-start.6
  743.6 575.8 %reduce-scatter.9.cloned.1.call-start = ((), (), s32[]{:S(2)}) async-start(), calls=%async_computation.6 | async-start | bytes 294912 | tf_op jit(solution)/shard_map/reduce_scatter | solution.py:149
  756.7 135.9 %collective-permute-start.2 = (f32[1,256]{1,0:T(1,128)S(1)}, f32[1,256]{1,0:T(1,128)S(1)}, u32[]{:S(2)}, u32[]{:S(2)}) collective-permute-start(f32[1,256]{1,0:T(1,128)S(1)} %slice.80), channel_id=1, source_target_pairs={{0,8},{8,16},{16,24},{24,32},{32,40},{40,48},{48,56},{56,64},{64,7... | collective-permute-start | bytes 3080 | tf_op jit(solution)/shard_map/ppermute | solution.py:19
  893.6 136.5 %collective-permute-start.3 = (f32[1,256]{1,0:T(1,128)S(1)}, f32[1,256]{1,0:T(1,128)S(1)}, u32[]{:S(2)}, u32[]{:S(2)}) collective-permute-start(f32[1,256]{1,0:T(1,128)S(1)} %slice.83), channel_id=1, source_target_pairs={{0,504},{8,0},{16,8},{24,16},{32,24},{40,32},{48,40},{56,48},{64,5... | collective-permute-start | bytes 3080 | tf_op jit(solution)/shard_map/ppermute | solution.py:19
  1163.1 152.2 %collective-permute-start.4 = (f32[1,256]{1,0:T(1,128)S(1)}, f32[1,256]{1,0:T(1,128)S(1)}, u32[]{:S(2)}, u32[]{:S(2)}) collective-permute-start(f32[1,256]{1,0:T(1,128)S(1)} %slice.84), channel_id=1, source_target_pairs={{0,8},{8,16},{16,24},{24,32},{32,40},{40,48},{48,56},{56,64},{64,7... | collective-permute-start | bytes 3080 | tf_op jit(solution)/shard_map/ppermute | solution.py:19
  1168.0 322.1 %reduce-scatter.11.cloned.1.call-start = ((), (), s32[]{:S(2)}) async-start(), calls=%async_computation.7 | async-start | bytes 294912 | tf_op jit(solution)/shard_map/reduce_scatter | solution.py:149
  1316.2 140.2 %collective-permute-start.5 = (f32[1,256]{1,0:T(1,128)S(1)}, f32[1,256]{1,0:T(1,128)S(1)}, u32[]{:S(2)}, u32[]{:S(2)}) collective-permute-start(f32[1,256]{1,0:T(1,128)S(1)} %slice.87), channel_id=1, source_target_pairs={{0,504},{8,0},{16,8},{24,16},{32,24},{40,32},{48,40},{56,48},{64,5... | collective-permute-start | bytes 3080 | tf_op jit(solution)/shard_map/ppermute | solution.py:19
Sparse Core Ops, SparseCore 0:
  40.4 42.1 reduce-scatter.4
  743.7 39.1 reduce-scatter.6
  1168.1 41.4 reduce-scatter.8
  1455.6 34.4 reduce-scatter.10
